TPU v7x, 32 devices: a whole 2x2x4 slice. The times are simulated.
32 devices in a mesh: section: 4 (over x, core), dp: 8 (over z, y).
Axes of the slice: x: 2, y: 2, z: 4, core: 2. Of those that a mesh axis runs over, the one named last changes fastest.
Arguments:
- embedded: bfloat16 [4, 256, 5120], P(None, 'dp'), may hold values from -6 to 6
- order: int32 [4], replicated, may hold values from 0 to 3, each once
- counts: int32 [4], P('section'), may hold values from 2 to 4, as said below
- gains: float32 [4, 4, 5120], P('section'), may hold values from 0.1 to 1.9
- mixers: bfloat16 [4, 4, 40, 128, 128], P('section'), may hold values from -0.5 to 0.5
- hidden_grads: bfloat16 [4, 4, 256, 13824], P('section', None, 'dp'), may hold values from -6 to 6
Outputs:
- input_factor: float32 [4, 64, 5120], P('section', 'dp')
- hidden_factor: float32 [4, 64, 13824], P('section', 'dp')
Inputs may be any that keep to these rules, and one draw needn't show every extreme that they name: order is a permutation of the roster positions. `counts`: some section has exactly 4 layers.
All inputs are finite; a program needn't handle non-finite values.
Results may differ from a plain program's by a relative error of at most 0.0069.
Values may be sent and summed in bfloat16 or wider, within the bound.
A program may use at most 128 MiB of HBM per device.

v0:
```python
import jax
import jax.numpy as jnp
import numpy as np
from jax import lax
from jax.sharding import PartitionSpec as P

MICRO = 4
A_ROWS_DEV = 8
G_ROWS_DEV = 8


def from_behind(value, axis, steps):
    count = lax.axis_size(axis)
    first, last = (max(0, -steps), min(count, count - steps))
    return lax.ppermute(value, axis, [(source, source + steps) for source in range(first, last)])


def normalize(values):
    return values * lax.rsqrt(jnp.mean(values * values, axis=-1, keepdims=True) + 1e-05)


def run_layers(hidden_in, count, gains, mixers):
    current = hidden_in.astype(jnp.float32)
    tokens_here, width = current.shape
    heads_count, head_size = (mixers.shape[1], mixers.shape[2])
    for layer_index in range(mixers.shape[0]):
        scaled = (normalize(current) * gains[layer_index]).astype(jnp.bfloat16)
        mixed = jnp.einsum(
            "thi,hij->thj",
            scaled.reshape(tokens_here, heads_count, head_size),
            mixers[layer_index],
            preferred_element_type=jnp.float32,
        )
        current = jnp.where(
            layer_index < count, current + mixed.reshape(tokens_here, width), current
        )
    return current.astype(jnp.bfloat16)


def weighted_gram(left_block, right_block, weights, inverse):
    total = None
    for micro_index in range(left_block.shape[0]):
        term = (
            jnp.dot(
                left_block[micro_index].T,
                right_block[micro_index],
                preferred_element_type=jnp.float32,
            )
            * weights[micro_index]
        )
        total = term if total is None else total + term
    return total * inverse


def body(embedded, order, counts, gains, mixers, hidden_grads):
    micro_count, tok_local, width = embedded.shape
    data_size = lax.axis_size("dp")
    inverse = 1.0 / (tok_local * data_size)
    section_index = lax.axis_index("section")
    my_count = counts[0]
    my_gains = gains[0]
    my_mixers = mixers[0]
    position_weight = jnp.asarray(0.95 ** (MICRO - 1 - np.arange(MICRO)), jnp.float32)
    onehot = (order[:, None] == jnp.arange(MICRO, dtype=jnp.int32)[None, :]).astype(jnp.float32)
    batch_weight = jnp.dot(position_weight, onehot)

    def advance(position, carry):
        outgoing, stash = carry
        incoming = from_behind(outgoing, "section", 1)
        slot = position - section_index
        valid = jnp.logical_and(slot >= 0, slot < micro_count)
        clipped = jnp.clip(slot, 0, micro_count - 1)
        picked = lax.dynamic_index_in_dim(order, clipped, 0, keepdims=False)
        first_input = lax.dynamic_index_in_dim(embedded, picked, 0, keepdims=False)
        section_input = jnp.where(section_index == 0, first_input, incoming)
        produced = run_layers(section_input, my_count, my_gains, my_mixers)
        normed = normalize(produced.astype(jnp.float32)).astype(jnp.bfloat16)
        previous = lax.dynamic_index_in_dim(stash, clipped, 0, keepdims=False)
        stash = lax.dynamic_update_index_in_dim(
            stash, jnp.where(valid, normed, previous), clipped, 0
        )
        return (produced, stash)

    start_carry = (
        jnp.zeros((tok_local, width), jnp.bfloat16),
        jnp.zeros((micro_count, tok_local, width), jnp.bfloat16),
    )
    total_steps = micro_count + lax.axis_size("section") - 1
    final_out, stash = lax.fori_loop(0, total_steps, advance, start_carry)
    a_rows = A_ROWS_DEV * data_size
    left_input = stash[:, :, :a_rows]
    columns = left_input
    input_factor = lax.psum_scatter(
        weighted_gram(columns, stash, position_weight, inverse),
        "dp",
        scatter_dimension=0,
        tiled=True,
    )
    grads = hidden_grads[0]
    g_rows = G_ROWS_DEV * data_size
    left_hidden = grads[:, :, :g_rows]
    columns = left_hidden
    hidden_factor = lax.psum_scatter(
        weighted_gram(columns, grads, batch_weight, inverse), "dp", scatter_dimension=0, tiled=True
    )
    return (input_factor[None], hidden_factor[None])


def solution(mesh):
    placed = (
        P(None, "dp", None),
        P(),
        P("section"),
        P("section", None, None),
        P("section", None, None, None, None),
        P("section", None, "dp", None),
    )
    return jax.shard_map(
        body,
        mesh=mesh,
        in_specs=placed,
        out_specs=(P("section", "dp", None), P("section", "dp", None)),
        check_vma=False,
    )
```

profile of v0, /device:TPU:0, one launch (start us, length us, event | category | flops | bytes accessed | tf_op | source)
XLA Modules:
  0.0 281.6 jit_solution(18348974735233897083)
XLA Ops:
  8.1 110.8 %while.18 = (s32[]{:T(128)}, bf16[32,5120]{1,0:T(8,128)(2,1)S(1)}, bf16[4,32,5120]{2,1,0:T(8,128)(2,1)S(1)}, pred[]{:T(512)}, pred[]{:T(512)}, /*index=5*/pred[]...) while((s32[]{:T(128)}, bf16[32,5120]{1,0:T(8,128)(2,1)S(1)}, ...), condition=%wide.region_6.7_spmd.clone, body=%wide.region_0.6_spmd.clone.sunk | while | flops 175472800 | bytes 43176416 | solution.py:89
  8.1 2.4 collective-permute-start
  10.5 0.6 dynamic_slice.38
  13.1 1.2 fusion.122
  14.3 1.8 fusion.123
  16.4 2.0 fusion.124
  18.6 0.6 copy-done
  21.0 5.9 %collective-permute-start = (bf16[32,5120]{1,0:T(8,128)(2,1)S(1)}, bf16[32,5120]{1,0:T(8,128)(2,1)S(1)}, u32[]{:S(2)}, u32[]{:S(2)}) collective-permute-start(bf16[32,5120]{1,0:T(8,128)(2,1)S(1)} %broadcast_select_fusion.2), channel_id=1, source_target_pairs={{0,8},{8,16},{16,24},{1,9},{9,17},{17,25},{2,10},{10,18},{18,26},{... | collective-permute-start | bytes 983048 | tf_op jit(solution)/shard_map/while/body/eval_jaxpr/ppermute | solution.py:15
  26.9 0.6 dynamic_slice.38
  29.5 1.2 fusion.122
  30.7 1.8 fusion.123
  32.8 2.0 fusion.124
  35.0 0.6 copy-done
  37.4 5.8 %collective-permute-start = (bf16[32,5120]{1,0:T(8,128)(2,1)S(1)}, bf16[32,5120]{1,0:T(8,128)(2,1)S(1)}, u32[]{:S(2)}, u32[]{:S(2)}) collective-permute-start(bf16[32,5120]{1,0:T(8,128)(2,1)S(1)} %broadcast_select_fusion.2), channel_id=1, source_target_pairs={{0,8},{8,16},{16,24},{1,9},{9,17},{17,25},{2,10},{10,18},{18,26},{... | collective-permute-start | bytes 983048 | tf_op jit(solution)/shard_map/while/body/eval_jaxpr/ppermute | solution.py:15
  45.8 1.2 fusion.122
  47.0 1.8 fusion.123
  49.1 2.0 fusion.124
  51.3 0.6 copy-done
  53.7 5.8 %collective-permute-start = (bf16[32,5120]{1,0:T(8,128)(2,1)S(1)}, bf16[32,5120]{1,0:T(8,128)(2,1)S(1)}, u32[]{:S(2)}, u32[]{:S(2)}) collective-permute-start(bf16[32,5120]{1,0:T(8,128)(2,1)S(1)} %broadcast_select_fusion.2), channel_id=1, source_target_pairs={{0,8},{8,16},{16,24},{1,9},{9,17},{17,25},{2,10},{10,18},{18,26},{... | collective-permute-start | bytes 983048 | tf_op jit(solution)/shard_map/while/body/eval_jaxpr/ppermute | solution.py:15
  59.5 0.6 dynamic_slice.38
  62.1 1.2 fusion.122
  63.3 1.8 fusion.123
  65.4 2.0 fusion.124
  67.6 0.6 copy-done
  70.0 5.8 %collective-permute-start = (bf16[32,5120]{1,0:T(8,128)(2,1)S(1)}, bf16[32,5120]{1,0:T(8,128)(2,1)S(1)}, u32[]{:S(2)}, u32[]{:S(2)}) collective-permute-start(bf16[32,5120]{1,0:T(8,128)(2,1)S(1)} %broadcast_select_fusion.2), channel_id=1, source_target_pairs={{0,8},{8,16},{16,24},{1,9},{9,17},{17,25},{2,10},{10,18},{18,26},{... | collective-permute-start | bytes 983048 | tf_op jit(solution)/shard_map/while/body/eval_jaxpr/ppermute | solution.py:15
  75.8 0.6 dynamic_slice.38
  78.4 1.2 fusion.122
  79.6 1.8 fusion.123
  81.7 2.0 fusion.124
  83.9 0.6 copy-done
  86.3 5.8 %collective-permute-start = (bf16[32,5120]{1,0:T(8,128)(2,1)S(1)}, bf16[32,5120]{1,0:T(8,128)(2,1)S(1)}, u32[]{:S(2)}, u32[]{:S(2)}) collective-permute-start(bf16[32,5120]{1,0:T(8,128)(2,1)S(1)} %broadcast_select_fusion.2), channel_id=1, source_target_pairs={{0,8},{8,16},{16,24},{1,9},{9,17},{17,25},{2,10},{10,18},{18,26},{... | collective-permute-start | bytes 983048 | tf_op jit(solution)/shard_map/while/body/eval_jaxpr/ppermute | solution.py:15
  94.7 1.2 fusion.122
  95.9 1.8 fusion.123
  98.0 2.0 fusion.124
  100.2 0.6 copy-done
  102.6 5.8 %collective-permute-start = (bf16[32,5120]{1,0:T(8,128)(2,1)S(1)}, bf16[32,5120]{1,0:T(8,128)(2,1)S(1)}, u32[]{:S(2)}, u32[]{:S(2)}) collective-permute-start(bf16[32,5120]{1,0:T(8,128)(2,1)S(1)} %broadcast_select_fusion.2), channel_id=1, source_target_pairs={{0,8},{8,16},{16,24},{1,9},{9,17},{17,25},{2,10},{10,18},{18,26},{... | collective-permute-start | bytes 983048 | tf_op jit(solution)/shard_map/while/body/eval_jaxpr/ppermute | solution.py:15
  111.0 1.2 fusion.122
  112.2 1.8 fusion.123
  114.3 2.0 fusion.124
  116.5 0.6 copy-done
  119.9 1.4 fusion.49
  122.2 0.7 fusion.79
  122.9 2.9 %convolution_multiply_fusion = f32[64,13824]{1,0:T(8,128)S(1)} fusion(f32[]{:T(128)} %bitcast.29, bf16[1,4,32,13824]{3,2,1,0:T(8,128)(2,1)} %param.14, bf16[4,32,13824]{2,1,0:T(8,128)(2,1)} %bitcast.210), kind=kOutput, calls=%fused_computation.60 | convolution fusion | flops 57507840 | bytes 4432384 | tf_op jit(solution)/shard_map/dot_general | solution.py:44
  125.7 1.2 convolution_multiply_fusion.1
  127.0 1.3 convolution_multiply_fusion.2
  128.2 3.3 %fusion.48 = f32[64,13824]{1,0:T(8,128)} fusion(f32[64,13824]{1,0:T(8,128)S(1)} %convolution_multiply_fusion, f32[64,13824]{1,0:T(8,128)S(1)} %convolution_multiply_fusion.1, f32[64,13824]{1,0:T(8,128)S(1)} %convolution_multiply_fusion.2, f32[]{:T(128)} %bitcast.20, bf16[1,4,32,13824]{3,2,1,0:T(8,128)(2,1)S(1)} %copy-done.1, ...), kind=kOutput, calls=%fused_computation.67 | convolution fusion | flops 61046784 | bytes 15048708 | tf_op jit(solution)/shard_map/dot_general | solution.py:44
  131.6 60.4 %reduce-scatter.3.cloned.1.call-done = f32[8,5120]{1,0:T(8,128)} async-done(((f32[64,5120]{1,0:T(8,128)}), f32[8,5120]{1,0:T(8,128)}) %reduce-scatter.3.cloned.1.call-update) | async-done | bytes 163856 | tf_op jit(solution)/shard_map/reduce_scatter | solution.py:93
  192.0 82.7 %reduce-scatter.5.cloned.1.call-done = f32[8,13824]{1,0:T(8,128)} async-done(((f32[64,13824]{1,0:T(8,128)}), f32[8,13824]{1,0:T(8,128)}) %reduce-scatter.5.cloned.1.call-update) | async-done | bytes 442384 | tf_op jit(solution)/shard_map/reduce_scatter | solution.py:103
  (140 shorter events, 20.0 us)
Async XLA Ops:
  7.2 0.9 copy-start.3
  7.2 0.9 copy-start.2
  7.2 184.8 %reduce-scatter.3.cloned.1.call-start = ((), (), s32[]{:S(2)}) async-start(), calls=%async_computation.2 | async-start | bytes 1474560 | tf_op jit(solution)/shard_map/reduce_scatter | solution.py:93
  8.1 5.0 %collective-permute-start = (bf16[32,5120]{1,0:T(8,128)(2,1)S(1)}, bf16[32,5120]{1,0:T(8,128)(2,1)S(1)}, u32[]{:S(2)}, u32[]{:S(2)}) collective-permute-start(bf16[32,5120]{1,0:T(8,128)(2,1)S(1)} %broadcast_select_fusion.2), channel_id=1, source_target_pairs={{0,8},{8,16},{16,24},{1,9},{9,17},{17,25},{2,10},{10,18},{18,26},{... | collective-permute-start | bytes 983048 | tf_op jit(solution)/shard_map/while/body/eval_jaxpr/ppermute | solution.py:15
  16.4 2.9 %copy-start = (bf16[4,40,128,128]{3,2,1,0:T(8,128)(2,1)S(1)}, bf16[4,40,128,128]{3,2,1,0:T(8,128)(2,1)}, u32[]{:S(2)}) copy-start(bf16[4,40,128,128]{3,2,1,0:T(8,128)(2,1)} %get-tuple-element.469) | copy-start | bytes 15728644 | tf_op jit(solution)/shard_map/while
  21.0 8.5 %collective-permute-start = (bf16[32,5120]{1,0:T(8,128)(2,1)S(1)}, bf16[32,5120]{1,0:T(8,128)(2,1)S(1)}, u32[]{:S(2)}, u32[]{:S(2)}) collective-permute-start(bf16[32,5120]{1,0:T(8,128)(2,1)S(1)} %broadcast_select_fusion.2), channel_id=1, source_target_pairs={{0,8},{8,16},{16,24},{1,9},{9,17},{17,25},{2,10},{10,18},{18,26},{... | collective-permute-start | bytes 983048 | tf_op jit(solution)/shard_map/while/body/eval_jaxpr/ppermute | solution.py:15
  32.8 2.9 %copy-start = (bf16[4,40,128,128]{3,2,1,0:T(8,128)(2,1)S(1)}, bf16[4,40,128,128]{3,2,1,0:T(8,128)(2,1)}, u32[]{:S(2)}) copy-start(bf16[4,40,128,128]{3,2,1,0:T(8,128)(2,1)} %get-tuple-element.469) | copy-start | bytes 15728644 | tf_op jit(solution)/shard_map/while
  37.4 8.4 %collective-permute-start = (bf16[32,5120]{1,0:T(8,128)(2,1)S(1)}, bf16[32,5120]{1,0:T(8,128)(2,1)S(1)}, u32[]{:S(2)}, u32[]{:S(2)}) collective-permute-start(bf16[32,5120]{1,0:T(8,128)(2,1)S(1)} %broadcast_select_fusion.2), channel_id=1, source_target_pairs={{0,8},{8,16},{16,24},{1,9},{9,17},{17,25},{2,10},{10,18},{18,26},{... | collective-permute-start | bytes 983048 | tf_op jit(solution)/shard_map/while/body/eval_jaxpr/ppermute | solution.py:15
  49.1 2.9 %copy-start = (bf16[4,40,128,128]{3,2,1,0:T(8,128)(2,1)S(1)}, bf16[4,40,128,128]{3,2,1,0:T(8,128)(2,1)}, u32[]{:S(2)}) copy-start(bf16[4,40,128,128]{3,2,1,0:T(8,128)(2,1)} %get-tuple-element.469) | copy-start | bytes 15728644 | tf_op jit(solution)/shard_map/while
  53.7 8.4 %collective-permute-start = (bf16[32,5120]{1,0:T(8,128)(2,1)S(1)}, bf16[32,5120]{1,0:T(8,128)(2,1)S(1)}, u32[]{:S(2)}, u32[]{:S(2)}) collective-permute-start(bf16[32,5120]{1,0:T(8,128)(2,1)S(1)} %broadcast_select_fusion.2), channel_id=1, source_target_pairs={{0,8},{8,16},{16,24},{1,9},{9,17},{17,25},{2,10},{10,18},{18,26},{... | collective-permute-start | bytes 983048 | tf_op jit(solution)/shard_map/while/body/eval_jaxpr/ppermute | solution.py:15
  65.4 2.9 %copy-start = (bf16[4,40,128,128]{3,2,1,0:T(8,128)(2,1)S(1)}, bf16[4,40,128,128]{3,2,1,0:T(8,128)(2,1)}, u32[]{:S(2)}) copy-start(bf16[4,40,128,128]{3,2,1,0:T(8,128)(2,1)} %get-tuple-element.469) | copy-start | bytes 15728644 | tf_op jit(solution)/shard_map/while
  70.0 8.4 %collective-permute-start = (bf16[32,5120]{1,0:T(8,128)(2,1)S(1)}, bf16[32,5120]{1,0:T(8,128)(2,1)S(1)}, u32[]{:S(2)}, u32[]{:S(2)}) collective-permute-start(bf16[32,5120]{1,0:T(8,128)(2,1)S(1)} %broadcast_select_fusion.2), channel_id=1, source_target_pairs={{0,8},{8,16},{16,24},{1,9},{9,17},{17,25},{2,10},{10,18},{18,26},{... | collective-permute-start | bytes 983048 | tf_op jit(solution)/shard_map/while/body/eval_jaxpr/ppermute | solution.py:15
  81.7 2.9 %copy-start = (bf16[4,40,128,128]{3,2,1,0:T(8,128)(2,1)S(1)}, bf16[4,40,128,128]{3,2,1,0:T(8,128)(2,1)}, u32[]{:S(2)}) copy-start(bf16[4,40,128,128]{3,2,1,0:T(8,128)(2,1)} %get-tuple-element.469) | copy-start | bytes 15728644 | tf_op jit(solution)/shard_map/while
  86.3 8.4 %collective-permute-start = (bf16[32,5120]{1,0:T(8,128)(2,1)S(1)}, bf16[32,5120]{1,0:T(8,128)(2,1)S(1)}, u32[]{:S(2)}, u32[]{:S(2)}) collective-permute-start(bf16[32,5120]{1,0:T(8,128)(2,1)S(1)} %broadcast_select_fusion.2), channel_id=1, source_target_pairs={{0,8},{8,16},{16,24},{1,9},{9,17},{17,25},{2,10},{10,18},{18,26},{... | collective-permute-start | bytes 983048 | tf_op jit(solution)/shard_map/while/body/eval_jaxpr/ppermute | solution.py:15
  98.0 2.9 %copy-start = (bf16[4,40,128,128]{3,2,1,0:T(8,128)(2,1)S(1)}, bf16[4,40,128,128]{3,2,1,0:T(8,128)(2,1)}, u32[]{:S(2)}) copy-start(bf16[4,40,128,128]{3,2,1,0:T(8,128)(2,1)} %get-tuple-element.469) | copy-start | bytes 15728644 | tf_op jit(solution)/shard_map/while
  102.6 8.4 %collective-permute-start = (bf16[32,5120]{1,0:T(8,128)(2,1)S(1)}, bf16[32,5120]{1,0:T(8,128)(2,1)S(1)}, u32[]{:S(2)}, u32[]{:S(2)}) collective-permute-start(bf16[32,5120]{1,0:T(8,128)(2,1)S(1)} %broadcast_select_fusion.2), channel_id=1, source_target_pairs={{0,8},{8,16},{16,24},{1,9},{9,17},{17,25},{2,10},{10,18},{18,26},{... | collective-permute-start | bytes 983048 | tf_op jit(solution)/shard_map/while/body/eval_jaxpr/ppermute | solution.py:15
  114.3 2.9 %copy-start = (bf16[4,40,128,128]{3,2,1,0:T(8,128)(2,1)S(1)}, bf16[4,40,128,128]{3,2,1,0:T(8,128)(2,1)}, u32[]{:S(2)}) copy-start(bf16[4,40,128,128]{3,2,1,0:T(8,128)(2,1)} %get-tuple-element.469) | copy-start | bytes 15728644 | tf_op jit(solution)/shard_map/while
  121.4 0.7 copy-start.4
  121.4 153.3 %reduce-scatter.5.cloned.1.call-start = ((), (), s32[]{:S(2)}) async-start(), calls=%async_computation.3 | async-start | bytes 3981312 | tf_op jit(solution)/shard_map/reduce_scatter | solution.py:103
  122.9 2.9 %copy-start.1 = (bf16[1,4,32,13824]{3,2,1,0:T(8,128)(2,1)S(1)}, bf16[1,4,32,13824]{3,2,1,0:T(8,128)(2,1)}, u32[]{:S(2)}) copy-start(bf16[1,4,32,13824]{3,2,1,0:T(8,128)(2,1)} %param.14) | copy-start | bytes 10616836
Sparse Core Ops, SparseCore 0:
  121.5 70.4 reduce-scatter.2
  196.2 78.4 reduce-scatter.4
where the time goes:
time: 283 us; the launch traced here: 282 us
  waiting for transfers between devices  143 us (51%)
  matrix products  45.2 us (16%)
  starting transfers between devices  37.3 us (13%)
  other arithmetic  16.7 us (6%)
  between operations  14.8 us (5%)
  loops' own time  13.7 us (5%)
  local copies, waits for them, and re-layouts  10.6 us (4%)
    reduce_scatter x1, waiting for transfers between devices, body(): lax.psum_scatter(weighted_gram(columns, grads, batch_weight, inverse), 'd...  82.7 us
    reduce_scatter x1, waiting for transfers between devices, body(): lax.psum_scatter(weighted_gram(columns, stash, position_weight, inverse),...  60.4 us
    ppermute x7, starting transfers between devices, from_behind(): lax.ppermute(value, axis, [(source, source + steps) for source in range(f...  37.2 us
    dot_general x28, matrix products, run_layers(): jnp.einsum('thi,hij->thj', scaled.reshape(tokens_here, heads_count, head_...  33.9 us
    reduce_sum x35, other arithmetic, normalize(): jnp.mean(values * values, axis=-1, keepdims=True) + 1e-05  14.9 us
    another operation x1, loops' own time, body(): final_out, stash = lax.fori_loop(0, total_steps, advance, start_carry)  13.7 us
    dot_general x8, matrix products, weighted_gram(): jnp.dot(left_block[micro_index].T, right_block[micro_index], preferred_el...  11.1 us
  transfers between devices with their start and end apart: 9, of which 2 were waited for; matrix products, arithmetic and copies ran while one was open for 5% of the time, Pallas kernels for 0%

commit v1 on v0

v1 whole, which is shorter than its diff:
```python
import functools

import jax
import jax.numpy as jnp
import numpy as np
from jax import lax
from jax.experimental import pallas as pl
from jax.experimental.pallas import tpu as pltpu
from jax.sharding import PartitionSpec as P

ROWS_DEV = 8
TILE = 256
HIDDEN_CHUNKS = 3
INPUT_CHUNKS = 2
MESH = pl.DeviceIdType.MESH
EPS = 1e-05


def kernel(
    sizes,
    emb_hbm, order_ref, counts_ref, gains_hbm, mixers_hbm, grads_hbm,
    out_in, out_hid,
    mixers, gains, gains_of, grads, arrived, produced, state, normed, acc, left_t,
    part_h, half_h, sum_h, got_h, part_i, half_i, sum_i, got_i,
    mixer_sem, gains_sem, grads_sem, emb_sem,
    relay_send, relay_recv,
    send1_h, recv1_h, send2_h, recv2_h, send1_i, recv1_i, send2_i, recv2_i,
):
    sections, data_size, micro_count, tokens, width, layers, heads, head_size, hidden = sizes
    peers = data_size // 2
    rows = ROWS_DEV * data_size
    inverse = 1.0 / (tokens * data_size)
    sec = lax.axis_index("section")
    dp = lax.axis_index("dp")
    mine, lane = lax.div(dp, 2), lax.rem(dp, 2)
    partner = mine * 2 + (1 - lane)

    def emb_copy(m):
        return pltpu.make_async_copy(emb_hbm.at[m], arrived.at[m], emb_sem.at[m])

    def mixer_copy(l):
        return pltpu.make_async_copy(mixers_hbm.at[0, l], mixers.at[l], mixer_sem.at[l])

    gains_copy = pltpu.make_async_copy(gains_hbm.at[0], gains, gains_sem)
    grads_copy = pltpu.make_async_copy(grads_hbm.at[0], grads, grads_sem)

    barrier = pltpu.get_barrier_semaphore()

    @pl.when(sec > 0)
    def _():
        pl.semaphore_signal(barrier, inc=1, device_id={"section": sec - 1}, device_id_type=MESH)

    @pl.when(sec < sections - 1)
    def _():
        pl.semaphore_signal(barrier, inc=1, device_id={"section": sec + 1}, device_id_type=MESH)

    pl.semaphore_signal(barrier, inc=1, device_id={"dp": partner}, device_id_type=MESH)
    for step in range(1, peers):
        other = lax.rem(mine + step, peers)
        pl.semaphore_signal(barrier, inc=1, device_id={"dp": other * 2 + lane}, device_id_type=MESH)

    @pl.when(sec == 0)
    def _():
        for m in range(micro_count):
            emb_copy(m).start()

    @pl.when(sec > 0)
    def _():
        grads_copy.start()

    gains_copy.start()
    for l in range(layers):
        mixer_copy(l).start()

    @pl.when(sec == 0)
    def _():
        grads_copy.start()

    position_weight = (0.95 ** (micro_count - 1 - np.arange(micro_count))).astype(np.float32)

    def batch_weight(m):
        total = jnp.float32(0.0)
        for k in range(micro_count):
            total = total + jnp.where(order_ref[k] == m, jnp.float32(position_weight[k]), jnp.float32(0.0))
        return total

    acc[...] = jnp.zeros_like(acc)
    links = (sec > 0).astype(jnp.int32) + (sec < sections - 1).astype(jnp.int32) + peers
    pl.semaphore_wait(barrier, links)

    def store_parts(part, k, offset, low, high):
        for j in range(data_size):
            at = slice(j * ROWS_DEV, (j + 1) * ROWS_DEV)
            block = jnp.concatenate([low[at], high[at]], axis=0).astype(jnp.bfloat16)
            part[k, j % 2, j // 2, :, pl.ds(offset, TILE)] = block

    def first_copy(part, half, send, recv, k):
        return pltpu.make_async_remote_copy(
            src_ref=part.at[k, 1 - lane], dst_ref=half.at[k],
            send_sem=send.at[k], recv_sem=recv.at[k],
            device_id={"dp": partner}, device_id_type=MESH,
        )

    def second_copy(total, got, send, recv, k, other):
        return pltpu.make_async_remote_copy(
            src_ref=total.at[k, other], dst_ref=got.at[k, mine],
            send_sem=send.at[k, other], recv_sem=recv.at[k, mine],
            device_id={"dp": other * 2 + lane}, device_id_type=MESH,
        )

    def second_arrival(total, got, send, recv, k, other):
        return pltpu.make_async_remote_copy(
            src_ref=total.at[k, other], dst_ref=got.at[k, other],
            send_sem=send.at[k, other], recv_sem=recv.at[k, other],
            device_id={"dp": other * 2 + lane}, device_id_type=MESH,
        )

    def pass_on(k, part, half, total, got, send1, recv1, send2, recv2):
        first_copy(part, half, send1, recv1, k).wait_recv()
        for step in range(1, peers + 1):
            other = lax.rem(mine + step, peers)
            both = part[k, lane, other].astype(jnp.float32) + half[k, other].astype(jnp.float32)
            total[k, other] = both.astype(jnp.bfloat16)
            if step < peers:
                second_copy(total, got, send2, recv2, k, other).start()

    def finish(k, out, part, half, total, got, send1, recv1, send2, recv2):
        chunk = part.shape[-1]
        middle = out.shape[-1] // 2
        summed = total[k, mine].astype(jnp.float32)
        for step in range(1, peers):
            other = lax.rem(mine + step, peers)
            second_arrival(total, got, send2, recv2, k, other).wait_recv()
            summed = summed + got[k, other].astype(jnp.float32)
        summed = summed * inverse
        out[0, :, pl.ds(k * chunk, chunk)] = summed[:ROWS_DEV]
        out[0, :, pl.ds(middle + k * chunk, chunk)] = summed[ROWS_DEV:]

    def drain(k, part, half, total, got, send1, recv1, send2, recv2):
        first_copy(part, half, send1, recv1, k).wait_send()
        for step in range(1, peers):
            other = lax.rem(mine + step, peers)
            second_copy(total, got, send2, recv2, k, other).wait_send()

    of_hidden = (part_h, half_h, sum_h, got_h, send1_h, recv1_h, send2_h, recv2_h)
    of_input = (part_i, half_i, sum_i, got_i, send1_i, recv1_i, send2_i, recv2_i)
    chunk_h, chunk_i = part_h.shape[-1], part_i.shape[-1]

    def hidden_left():
        grads_copy.wait()
        for m in range(micro_count):
            left = grads[m, :, :rows].astype(jnp.float32)
            left_t[m] = jnp.transpose(left).astype(jnp.bfloat16)

    def hidden_gram(k):
        weights = [batch_weight(m) for m in range(micro_count)]

        def tile(i, carry):
            offset = pl.multiple_of(i * TILE, TILE)
            start = pl.multiple_of(k * chunk_h + i * TILE, TILE)
            sums = []
            for at in (start, start + hidden // 2):
                total = None
                for m in range(micro_count):
                    term = jnp.dot(
                        left_t[m], grads[m, :, pl.ds(pl.multiple_of(at, TILE), TILE)],
                        preferred_element_type=jnp.float32,
                    ) * weights[m]
                    total = term if total is None else total + term
                sums.append(total)
            store_parts(part_h, k, offset, *sums)
            return carry

        lax.fori_loop(0, chunk_h // TILE, tile, 0)
        first_copy(part_h, half_h, send1_h, recv1_h, k).start()

    @pl.when(sec > 0)
    def _():
        hidden_left()

        def one(k, carry):
            hidden_gram(k)
            return carry

        lax.fori_loop(0, HIDDEN_CHUNKS, one, 0)

    gains_copy.wait()
    for l in range(layers):
        gains_of[l] = jnp.broadcast_to(gains[l:l + 1, :], (8, width))

    def relay_copy(m):
        return pltpu.make_async_remote_copy(
            src_ref=produced.at[m], dst_ref=arrived.at[m],
            send_sem=relay_send.at[m], recv_sem=relay_recv.at[m],
            device_id={"section": lax.rem(sec + 1, sections)}, device_id_type=MESH,
        )

    def scale_of(squares):
        return lax.rsqrt(jnp.sum(squares, axis=-1, keepdims=True) * (1.0 / width) + EPS)

    def columns(g):
        return slice(g * head_size, (g + 1) * head_size)

    def micro(m, carry):
        @pl.when(sec == 0)
        def _():
            emb_copy(m).wait()

        @pl.when(sec > 0)
        def _():
            relay_copy(m).wait_recv()

        squares = jnp.zeros((tokens, head_size), jnp.float32)
        for g in range(heads):
            value = arrived[m, :, columns(g)].astype(jnp.float32)
            state[:, columns(g)] = value
            squares = squares + value * value

        def layer(l, squares):
            @pl.when(m == 0)
            def _():
                mixer_copy(l).wait()

            active = jnp.where(l < counts_ref[0], jnp.float32(1.0), jnp.float32(0.0))
            scale = scale_of(squares) * active
            after = jnp.zeros((tokens, head_size), jnp.float32)
            for g in range(heads):
                value = state[:, columns(g)]
                scaled = ((value * scale) * gains_of[l, 0:1, columns(g)]).astype(jnp.bfloat16)
                value = value + jnp.dot(scaled, mixers[l, g], preferred_element_type=jnp.float32)
                state[:, columns(g)] = value
                after = after + value * value
            return after

        lax.fori_loop(0, layers, layer, squares)

        squares = jnp.zeros((tokens, head_size), jnp.float32)
        for g in range(heads):
            value = state[:, columns(g)].astype(jnp.bfloat16)
            produced[m, :, columns(g)] = value
            value = value.astype(jnp.float32)
            squares = squares + value * value

        @pl.when(sec < sections - 1)
        def _():
            relay_copy(m).start()

        scale = scale_of(squares)
        for g in range(heads):
            value = produced[m, :, columns(g)].astype(jnp.float32) * scale
            normed[:, columns(g)] = value.astype(jnp.bfloat16)
        left = jnp.transpose(normed[:, :rows].astype(jnp.float32)).astype(jnp.bfloat16)
        weight = batch_weight(m)
        for at in range(0, width, TILE):
            term = jnp.dot(left, normed[:, at:at + TILE], preferred_element_type=jnp.float32)
            acc[:, at:at + TILE] += term * weight

        @pl.when(jnp.logical_and(sec == 0, m < HIDDEN_CHUNKS))
        def _():
            @pl.when(m == 0)
            def _():
                hidden_left()

            hidden_gram(m)

        @pl.when(jnp.logical_and(sec * 2 >= sections, m < HIDDEN_CHUNKS))
        def _():
            pass_on(m, *of_hidden)

        return carry

    lax.fori_loop(0, micro_count, micro, 0)

    for k in range(INPUT_CHUNKS):
        for i in range(chunk_i // TILE):
            at = k * chunk_i + i * TILE
            middle = at + width // 2
            store_parts(part_i, k, i * TILE, acc[:, at:at + TILE], acc[:, middle:middle + TILE])
        first_copy(part_i, half_i, send1_i, recv1_i, k).start()

    @pl.when(sec * 2 < sections)
    def _():
        def one(k, carry):
            pass_on(k, *of_hidden)
            return carry

        lax.fori_loop(0, HIDDEN_CHUNKS, one, 0)

    for k in range(INPUT_CHUNKS):
        pass_on(k, *of_input)
    for k in range(HIDDEN_CHUNKS):
        finish(k, out_hid, *of_hidden)
    for k in range(INPUT_CHUNKS):
        finish(k, out_in, *of_input)

    for k in range(HIDDEN_CHUNKS):
        drain(k, *of_hidden)
    for k in range(INPUT_CHUNKS):
        drain(k, *of_input)

    @pl.when(sec < sections - 1)
    def _():
        for m in range(micro_count):
            relay_copy(m).wait_send()


def body(embedded, order, counts, gains, mixers, hidden_grads):
    micro_count, tokens, width = embedded.shape
    _, layers, heads, head_size, _ = mixers.shape
    hidden = hidden_grads.shape[-1]
    sections, data_size = lax.axis_size("section"), lax.axis_size("dp")
    sizes = (sections, data_size, micro_count, tokens, width, layers, heads, head_size, hidden)
    peers = data_size // 2
    rows = ROWS_DEV * data_size

    def buffers(columns, chunks):
        chunk = columns // 2 // chunks
        tile = (2 * ROWS_DEV, chunk)
        return [
            pltpu.VMEM((chunks, 2, peers) + tile, jnp.bfloat16),
            pltpu.VMEM((chunks, peers) + tile, jnp.bfloat16),
            pltpu.VMEM((chunks, peers) + tile, jnp.bfloat16),
            pltpu.VMEM((chunks, peers) + tile, jnp.bfloat16),
        ]

    def semaphores(chunks):
        return [
            pltpu.SemaphoreType.DMA((chunks,)),
            pltpu.SemaphoreType.DMA((chunks,)),
            pltpu.SemaphoreType.DMA((chunks, peers)),
            pltpu.SemaphoreType.DMA((chunks, peers)),
        ]

    anywhere = pl.BlockSpec(memory_space=pl.ANY)
    scalars = pl.BlockSpec(memory_space=pltpu.SMEM)
    vmem = pl.BlockSpec(memory_space=pltpu.VMEM)
    return pl.pallas_call(
        functools.partial(kernel, sizes),
        out_shape=(
            jax.ShapeDtypeStruct((1, ROWS_DEV, width), jnp.float32),
            jax.ShapeDtypeStruct((1, ROWS_DEV, hidden), jnp.float32),
        ),
        in_specs=[anywhere, scalars, scalars, anywhere, anywhere, anywhere],
        out_specs=(vmem, vmem),
        scratch_shapes=[
            pltpu.VMEM((layers, heads, head_size, head_size), jnp.bfloat16),
            pltpu.VMEM((layers, width), jnp.float32),
            pltpu.VMEM((layers, 8, width), jnp.float32),
            pltpu.VMEM((micro_count, tokens, hidden), jnp.bfloat16),
            pltpu.VMEM((micro_count, tokens, width), jnp.bfloat16),
            pltpu.VMEM((micro_count, tokens, width), jnp.bfloat16),
            pltpu.VMEM((tokens, width), jnp.float32),
            pltpu.VMEM((tokens, width), jnp.bfloat16),
            pltpu.VMEM((rows, width), jnp.float32),
            pltpu.VMEM((micro_count, rows, tokens), jnp.bfloat16),
        ]
        + buffers(hidden, HIDDEN_CHUNKS)
        + buffers(width, INPUT_CHUNKS)
        + [
            pltpu.SemaphoreType.DMA((layers,)),
            pltpu.SemaphoreType.DMA,
            pltpu.SemaphoreType.DMA,
            pltpu.SemaphoreType.DMA((micro_count,)),
            pltpu.SemaphoreType.DMA((micro_count,)),
            pltpu.SemaphoreType.DMA((micro_count,)),
        ]
        + semaphores(HIDDEN_CHUNKS)
        + semaphores(INPUT_CHUNKS),
        compiler_params=pltpu.CompilerParams(
            collective_id=0, has_side_effects=True, vmem_limit_bytes=56 * 1024 * 1024
        ),
    )(embedded, order, counts, gains, mixers, hidden_grads)


def solution(mesh):
    placed = (
        P(None, "dp", None),
        P(),
        P("section"),
        P("section", None, None),
        P("section", None, None, None, None),
        P("section", None, "dp", None),
    )
    return jax.shard_map(
        body,
        mesh=mesh,
        in_specs=placed,
        out_specs=(P("section", "dp", None), P("section", "dp", None)),
        check_vma=False,
    )
```

time: 283 us -> 57 us (0.20)
  the two profiles are of different devices: /device:TPU:0 before, /device:TPU:1 now
where the time goes in v1:
time: 57 us; the launch traced here: 56.8 us
  Pallas kernels  52.1 us (91%)
  local copies, waits for them, and re-layouts  3.4 us (6%)
  between operations  1.28 us (2%)
    pallas_call x1, Pallas kernels, body(): pl.pallas_call(functools.partial(kernel, sizes), out_shape=(jax.ShapeDtyp...  52.1 us
    unnamed x2, local copies, waits for them, and re-layouts  3.4 us

profile of v1, /device:TPU:1, one launch (start us, length us, event | category | flops | bytes accessed | tf_op | source)
XLA Modules:
  0.0 56.8 jit_solution(5269317562842740719)
XLA Ops:
  1.3 52.1 %shard_map.77 = (f32[1,8,5120]{2,1,0:T(8,128)}, f32[1,8,13824]{2,1,0:T(8,128)}) custom-call(bf16[4,32,5120]{2,1,0:T(8,128)(2,1)} %emb_hbm.1, s32[4]{0:T(128)} %order_ref.1, s32[1]{0:T(128)S(6)} %copy.10.counts_ref, f32[1,4,5120]{2,1,0:T(4,128)} %gains_hbm.1, bf16[1,4,40,128,128]{4,3,2,1,0:T(8,128)(2,1)} %mixers_hbm.1, bf16[1,4,32,13824]{3,2,1,0:T(8,128)(2,1)} %grads_hbm.1), custom_call_target="tpu_custom_call" | custom-call | tf_op jit(solution)/shard_map/pallas_call | solution.py:337
  53.4 1.6 %copy.11 = f32[1,8,5120]{2,1,0:T(8,128)} copy(f32[1,8,5120]{2,1,0:T(8,128)} %get-tuple-element.4) | data formatting | bytes 327680
  55.0 1.8 %copy.12 = f32[1,8,13824]{2,1,0:T(8,128)} copy(f32[1,8,13824]{2,1,0:T(8,128)} %get-tuple-element.5) | data formatting | bytes 884736

commit v2 on v1

--- a/solution.py
+++ b/solution.py
@@ -20,7 +20,7 @@
     sizes,
     emb_hbm, order_ref, counts_ref, gains_hbm, mixers_hbm, grads_hbm,
     out_in, out_hid,
-    mixers, gains, gains_of, grads, arrived, produced, state, normed, acc, left_t,
+    mixers, gains, gains_of, grads, arrived, produced, state, squared, normed, acc, left_t,
     part_h, half_h, sum_h, got_h, part_i, half_i, sum_i, got_i,
     mixer_sem, gains_sem, grads_sem, emb_sem,
     relay_send, relay_recv,
@@ -174,15 +174,22 @@
         lax.fori_loop(0, chunk_h // TILE, tile, 0)
         first_copy(part_h, half_h, send1_h, recv1_h, k).start()
 
+    early = sec * 2 < sections
+    before = jnp.where(sec == 0, 0, jnp.where(early, HIDDEN_CHUNKS - 1, HIDDEN_CHUNKS))
+    passed = jnp.where(sec == 0, 0, jnp.where(early, 1, jnp.where(sec == sections - 1, HIDDEN_CHUNKS, HIDDEN_CHUNKS - 1)))
+
+    def hidden_part(k, carry):
+        hidden_gram(k)
+        return carry
+
+    def pass_hidden(k, carry):
+        pass_on(k, *of_hidden)
+        return carry
+
     @pl.when(sec > 0)
     def _():
         hidden_left()
-
-        def one(k, carry):
-            hidden_gram(k)
-            return carry
-
-        lax.fori_loop(0, HIDDEN_CHUNKS, one, 0)
+        lax.fori_loop(0, before, hidden_part, 0)
 
     gains_copy.wait()
     for l in range(layers):
@@ -241,11 +248,24 @@
             value = value.astype(jnp.float32)
             squares = squares + value * value
 
+        squared[m] = squares
+
         @pl.when(sec < sections - 1)
         def _():
             relay_copy(m).start()
 
-        scale = scale_of(squares)
+        @pl.when(jnp.logical_not(early))
+        def _():
+            statistics(m)
+
+        @pl.when(jnp.logical_and(jnp.logical_not(early), m < passed))
+        def _():
+            pass_on(m, *of_hidden)
+
+        return carry
+
+    def statistics(m):
+        scale = scale_of(squared[m])
         for g in range(heads):
             value = produced[m, :, columns(g)].astype(jnp.float32) * scale
             normed[:, columns(g)] = value.astype(jnp.bfloat16)
@@ -255,21 +275,17 @@
             term = jnp.dot(left, normed[:, at:at + TILE], preferred_element_type=jnp.float32)
             acc[:, at:at + TILE] += term * weight
 
-        @pl.when(jnp.logical_and(sec == 0, m < HIDDEN_CHUNKS))
-        def _():
-            @pl.when(m == 0)
-            def _():
-                hidden_left()
-
-            hidden_gram(m)
-
-        @pl.when(jnp.logical_and(sec * 2 >= sections, m < HIDDEN_CHUNKS))
-        def _():
-            pass_on(m, *of_hidden)
-
-        return carry
-
     lax.fori_loop(0, micro_count, micro, 0)
+
+    @pl.when(early)
+    def _():
+        @pl.when(sec == 0)
+        def _():
+            hidden_left()
+
+        lax.fori_loop(before, HIDDEN_CHUNKS, hidden_part, 0)
+        lax.fori_loop(0, passed, pass_hidden, 0)
+        lax.fori_loop(0, micro_count, lambda m, carry: (statistics(m), carry)[1], 0)
 
     for k in range(INPUT_CHUNKS):
         for i in range(chunk_i // TILE):
@@ -278,18 +294,12 @@
             store_parts(part_i, k, i * TILE, acc[:, at:at + TILE], acc[:, middle:middle + TILE])
         first_copy(part_i, half_i, send1_i, recv1_i, k).start()
 
-    @pl.when(sec * 2 < sections)
-    def _():
-        def one(k, carry):
-            pass_on(k, *of_hidden)
-            return carry
-
-        lax.fori_loop(0, HIDDEN_CHUNKS, one, 0)
-
+    lax.fori_loop(passed, HIDDEN_CHUNKS, pass_hidden, 0)
+    for k in range(HIDDEN_CHUNKS - 1):
+        finish(k, out_hid, *of_hidden)
     for k in range(INPUT_CHUNKS):
         pass_on(k, *of_input)
-    for k in range(HIDDEN_CHUNKS):
-        finish(k, out_hid, *of_hidden)
+    finish(HIDDEN_CHUNKS - 1, out_hid, *of_hidden)
     for k in range(INPUT_CHUNKS):
         finish(k, out_in, *of_input)
 
@@ -350,6 +360,7 @@
             pltpu.VMEM((micro_count, tokens, width), jnp.bfloat16),
             pltpu.VMEM((micro_count, tokens, width), jnp.bfloat16),
             pltpu.VMEM((tokens, width), jnp.float32),
+            pltpu.VMEM((micro_count, tokens, head_size), jnp.float32),
             pltpu.VMEM((tokens, width), jnp.bfloat16),
             pltpu.VMEM((rows, width), jnp.float32),
             pltpu.VMEM((micro_count, rows, tokens), jnp.bfloat16),

time: 57 us -> 55.1 us (0.967)
  the two profiles are of different devices: /device:TPU:1 before, /device:TPU:0 now
where the time goes in v2:
time: 55.1 us; the launch traced here: 54.9 us
  Pallas kernels  50.2 us (91%)
  local copies, waits for them, and re-layouts  3.4 us (6%)
  between operations  1.28 us (2%)
    pallas_call x1, Pallas kernels, body(): pl.pallas_call(functools.partial(kernel, sizes), out_shape=(jax.ShapeDtyp...  50.2 us
    unnamed x2, local copies, waits for them, and re-layouts  3.4 us

profile of v2, /device:TPU:0, one launch (start us, length us, event | category | flops | bytes accessed | tf_op | source)
XLA Modules:
  0.0 54.9 jit_solution(17005751906931408935)
XLA Ops:
  1.3 50.2 %shard_map.77 = (f32[1,8,5120]{2,1,0:T(8,128)}, f32[1,8,13824]{2,1,0:T(8,128)}) custom-call(bf16[4,32,5120]{2,1,0:T(8,128)(2,1)} %emb_hbm.1, s32[4]{0:T(128)} %order_ref.1, s32[1]{0:T(128)S(6)} %copy.10.counts_ref, f32[1,4,5120]{2,1,0:T(4,128)} %gains_hbm.1, bf16[1,4,40,128,128]{4,3,2,1,0:T(8,128)(2,1)} %mixers_hbm.1, bf16[1,4,32,13824]{3,2,1,0:T(8,128)(2,1)} %grads_hbm.1), custom_call_target="tpu_custom_call" | custom-call | tf_op jit(solution)/shard_map/pallas_call | solution.py:347
  51.5 1.6 %copy.11 = f32[1,8,5120]{2,1,0:T(8,128)} copy(f32[1,8,5120]{2,1,0:T(8,128)} %get-tuple-element.4) | data formatting | bytes 327680
  53.1 1.8 %copy.12 = f32[1,8,13824]{2,1,0:T(8,128)} copy(f32[1,8,13824]{2,1,0:T(8,128)} %get-tuple-element.5) | data formatting | bytes 884736

commit v3 on v2

--- a/solution.py
+++ b/solution.py
@@ -10,7 +10,7 @@
 
 ROWS_DEV = 8
 TILE = 256
-HIDDEN_CHUNKS = 3
+HIDDEN_CHUNKS = 9
 INPUT_CHUNKS = 2
 MESH = pl.DeviceIdType.MESH
 EPS = 1e-05
@@ -133,8 +133,8 @@
             second_arrival(total, got, send2, recv2, k, other).wait_recv()
             summed = summed + got[k, other].astype(jnp.float32)
         summed = summed * inverse
-        out[0, :, pl.ds(k * chunk, chunk)] = summed[:ROWS_DEV]
-        out[0, :, pl.ds(middle + k * chunk, chunk)] = summed[ROWS_DEV:]
+        out[0, :, pl.ds(pl.multiple_of(k * chunk, TILE), chunk)] = summed[:ROWS_DEV]
+        out[0, :, pl.ds(pl.multiple_of(middle + k * chunk, TILE), chunk)] = summed[ROWS_DEV:]
 
     def drain(k, part, half, total, got, send1, recv1, send2, recv2):
         first_copy(part, half, send1, recv1, k).wait_send()
@@ -175,8 +175,19 @@
         first_copy(part_h, half_h, send1_h, recv1_h, k).start()
 
     early = sec * 2 < sections
-    before = jnp.where(sec == 0, 0, jnp.where(early, HIDDEN_CHUNKS - 1, HIDDEN_CHUNKS))
-    passed = jnp.where(sec == 0, 0, jnp.where(early, 1, jnp.where(sec == sections - 1, HIDDEN_CHUNKS, HIDDEN_CHUNKS - 1)))
+    last = sec == sections - 1
+    first = sec == 0
+
+    def plan(at_first, at_early, at_late, at_last):
+        late = jnp.where(last, at_last, at_late)
+        return jnp.where(first, at_first, jnp.where(early, at_early, late))
+
+    before = plan(0, 6, HIDDEN_CHUNKS, HIDDEN_CHUNKS)
+    waiting, base, most = plan(0, 0, 2, 4), plan(0, 2, 3, 6), plan(0, 5, 7, HIDDEN_CHUNKS)
+    passed = plan(3, 6, 7, HIDDEN_CHUNKS)
+
+    def passed_by(m):
+        return jnp.where(m == 0, waiting, jnp.minimum(base + 2 * (m - 1), most))
 
     def hidden_part(k, carry):
         hidden_gram(k)
@@ -190,6 +201,7 @@
     def _():
         hidden_left()
         lax.fori_loop(0, before, hidden_part, 0)
+        lax.fori_loop(0, waiting, pass_hidden, 0)
 
     gains_copy.wait()
     for l in range(layers):
@@ -258,9 +270,15 @@
         def _():
             statistics(m)
 
-        @pl.when(jnp.logical_and(jnp.logical_not(early), m < passed))
+        @pl.when(jnp.logical_and(first, m > 0))
         def _():
-            pass_on(m, *of_hidden)
+            @pl.when(m == 1)
+            def _():
+                hidden_left()
+
+            lax.fori_loop(HIDDEN_CHUNKS // 3 * (m - 1), HIDDEN_CHUNKS // 3 * m, hidden_part, 0)
+
+        lax.fori_loop(passed_by(m), passed_by(m + 1), pass_hidden, 0)
 
         return carry
 
@@ -279,12 +297,8 @@
 
     @pl.when(early)
     def _():
-        @pl.when(sec == 0)
-        def _():
-            hidden_left()
-
-        lax.fori_loop(before, HIDDEN_CHUNKS, hidden_part, 0)
-        lax.fori_loop(0, passed, pass_hidden, 0)
+        lax.fori_loop(jnp.where(first, HIDDEN_CHUNKS, before), HIDDEN_CHUNKS, hidden_part, 0)
+        lax.fori_loop(most, passed, pass_hidden, 0)
         lax.fori_loop(0, micro_count, lambda m, carry: (statistics(m), carry)[1], 0)
 
     for k in range(INPUT_CHUNKS):
@@ -295,18 +309,31 @@
         first_copy(part_i, half_i, send1_i, recv1_i, k).start()
 
     lax.fori_loop(passed, HIDDEN_CHUNKS, pass_hidden, 0)
-    for k in range(HIDDEN_CHUNKS - 1):
+    def finish_hidden(k, carry):
         finish(k, out_hid, *of_hidden)
-    for k in range(INPUT_CHUNKS):
+        return carry
+
+    def pass_input(k, carry):
         pass_on(k, *of_input)
-    finish(HIDDEN_CHUNKS - 1, out_hid, *of_hidden)
-    for k in range(INPUT_CHUNKS):
+        return carry
+
+    def finish_input(k, carry):
         finish(k, out_in, *of_input)
-
-    for k in range(HIDDEN_CHUNKS):
+        return carry
+
+    def drain_hidden(k, carry):
         drain(k, *of_hidden)
-    for k in range(INPUT_CHUNKS):
+        return carry
+
+    def drain_input(k, carry):
         drain(k, *of_input)
+        return carry
+
+    lax.fori_loop(0, INPUT_CHUNKS, pass_input, 0)
+    lax.fori_loop(0, HIDDEN_CHUNKS, finish_hidden, 0)
+    lax.fori_loop(0, INPUT_CHUNKS, finish_input, 0)
+    lax.fori_loop(0, HIDDEN_CHUNKS, drain_hidden, 0)
+    lax.fori_loop(0, INPUT_CHUNKS, drain_input, 0)
 
     @pl.when(sec < sections - 1)
     def _():

time: 55.1 us -> 51.2 us (0.929)
  Pallas kernels: 50.2 us -> 46.3 us
    pallas_call x1, Pallas kernels: 50.2 us -> 46.3 us  [body(): pl.pallas_call(functools.partial(kernel, sizes), out_shape=(jax.ShapeDtyp...]
where the time goes in v3:
time: 51.2 us; the launch traced here: 51 us
  Pallas kernels  46.3 us (90%)
  local copies, waits for them, and re-layouts  3.4 us (7%)
  between operations  1.28 us (2%)
    pallas_call x1, Pallas kernels, body(): pl.pallas_call(functools.partial(kernel, sizes), out_shape=(jax.ShapeDtyp...  46.3 us
    unnamed x2, local copies, waits for them, and re-layouts  3.4 us

profile of v3, /device:TPU:0, one launch (start us, length us, event | category | flops | bytes accessed | tf_op | source)
XLA Modules:
  0.0 51.0 jit_solution(3719173898701143307)
XLA Ops:
  1.3 46.3 %shard_map.77 = (f32[1,8,5120]{2,1,0:T(8,128)}, f32[1,8,13824]{2,1,0:T(8,128)}) custom-call(bf16[4,32,5120]{2,1,0:T(8,128)(2,1)} %emb_hbm.1, s32[4]{0:T(128)} %order_ref.1, s32[1]{0:T(128)S(6)} %copy.10.counts_ref, f32[1,4,5120]{2,1,0:T(4,128)} %gains_hbm.1, bf16[1,4,40,128,128]{4,3,2,1,0:T(8,128)(2,1)} %mixers_hbm.1, bf16[1,4,32,13824]{3,2,1,0:T(8,128)(2,1)} %grads_hbm.1), custom_call_target="tpu_custom_call" | custom-call | tf_op jit(solution)/shard_map/pallas_call | solution.py:374
  47.6 1.6 %copy.11 = f32[1,8,5120]{2,1,0:T(8,128)} copy(f32[1,8,5120]{2,1,0:T(8,128)} %get-tuple-element.4) | data formatting | bytes 327680
  49.2 1.8 %copy.12 = f32[1,8,13824]{2,1,0:T(8,128)} copy(f32[1,8,13824]{2,1,0:T(8,128)} %get-tuple-element.5) | data formatting | bytes 884736
